TPU v7x, 512 devices: a whole 4x4x16 slice. The times are simulated.
512 devices in a mesh: grp: 8 (over y, core), mem: 64 (over x, z).
Axes of the slice: x: 4, y: 4, z: 16, core: 2. Of those that a mesh axis runs over, the one named last changes fastest.
Arguments:
- tokens: bfloat16 [65536, 1024], P(('grp', 'mem')), may hold values from -6 to 6
- cotangent: bfloat16 [65536, 1024], P(('grp', 'mem')), may hold values from -6 to 6
- path: int32 [512, 3], P(('grp', 'mem')), may hold values from 0 to 1023, as said below
- coarse_weights: bfloat16 [4, 1024, 512], P(None, 'mem'), may hold values from -0.1875 to 0.1875
- middle_weights: bfloat16 [64, 1024, 256], P(None, 'mem'), may hold values from -0.1875 to 0.1875
- fine_weights: bfloat16 [1024, 1024, 128], P('grp', 'mem'), may hold values from -0.1875 to 0.1875
Outputs:
- tokens_grad: bfloat16 [65536, 1024], P(('grp', 'mem'))
- coarse_grad: bfloat16 [4, 1024, 512], P(None, 'mem')
- middle_grad: bfloat16 [64, 1024, 256], P(None, 'mem')
- fine_grad: bfloat16 [1024, 1024, 128], P('grp', 'mem')
Inputs may be any that keep to these rules, and one draw needn't show every extreme that they name: Row d is the path of document d: column 0 its coarse block, column 1 its middle block, column 2 its fine block, with middle = fine * 64 // 1024 and coarse = middle * 4 // 64. Some fine blocks are chosen by many documents.
All inputs are finite; a program needn't handle non-finite values.
Results may differ from a plain program's by a relative error of at most 0.005.
Values may be sent and summed in bfloat16 or wider, within the bound.
No kernel may reach another device: no remote copies, remote signals or barrier semaphores. Data moves between devices by JAX's collectives and lax.ppermute only.
A program may use at most 64 MiB of HBM per device.

v0:
```python
from functools import partial
import jax
import jax.numpy as jnp
from jax import lax
from jax.sharding import PartitionSpec as P


def contract_rows(left, right):
    return lax.dot_general(
        left, right, (((0,), (0,)), ((), ())), preferred_element_type=jnp.float32
    )


def level_terms(inputs, upstream, weights):
    hidden_width = weights.shape[1] // 2
    up_half = weights[:, :hidden_width]
    down_half = weights[:, hidden_width:]
    before = jnp.dot(inputs, up_half, preferred_element_type=jnp.float32)
    hidden, pullback = jax.vjp(partial(jax.nn.gelu, approximate=True), before)
    hidden_low = hidden.astype(jnp.bfloat16)
    hidden_grad = jnp.dot(upstream, down_half, preferred_element_type=jnp.float32)
    before_grad = pullback(hidden_grad)[0].astype(jnp.bfloat16)
    up_grad = contract_rows(inputs, before_grad)
    down_grad = contract_rows(upstream, hidden_low)
    input_part = lax.dot_general(
        before_grad, up_half, (((1,), (1,)), ((), ())), preferred_element_type=jnp.float32
    )
    return (jnp.concatenate([up_grad, down_grad], axis=1), input_part)


def one_hot_rows(identity, count):
    return (identity[:, None] == jnp.arange(count, dtype=jnp.int32)[None, :]).astype(jnp.bfloat16)


def select_blocks(picker, blocks):
    return jnp.einsum("mk,krh->mrh", picker, blocks, preferred_element_type=jnp.float32).astype(
        jnp.bfloat16
    )


def collect_blocks(picker, pieces):
    return jnp.einsum(
        "mk,mrh->krh", picker.astype(jnp.float32), pieces, precision=lax.Precision.HIGHEST
    )


def on_device(tokens, cotangent, path, coarse_weights, middle_weights, fine_weights):
    member_count = lax.axis_size("mem")
    group_count = lax.axis_size("grp")
    group = lax.axis_index("grp")
    row_count = coarse_weights.shape[1]
    fine_owned = fine_weights.shape[0]
    route = path[0]
    all_paths = lax.all_gather(path, ("grp", "mem"), axis=0, tiled=True)
    group_paths = lax.dynamic_slice_in_dim(all_paths, group * member_count, member_count, 0)
    coarse_pick = one_hot_rows(group_paths[:, 0], coarse_weights.shape[0])
    middle_pick = one_hot_rows(group_paths[:, 1], middle_weights.shape[0])
    middle_send = select_blocks(middle_pick, middle_weights)
    every_block = lax.all_gather(coarse_weights, "mem", axis=1, tiled=True)
    coarse_block = lax.dynamic_index_in_dim(every_block, route[0], 0, keepdims=False)
    middle_block = lax.all_to_all(middle_send, "mem", split_axis=0, concat_axis=1, tiled=True)[0]
    offsets = all_paths[:, 2] - group * fine_owned
    fine_pick = one_hot_rows(offsets, fine_owned)
    fine_send = select_blocks(fine_pick, fine_weights).reshape(
        group_count, member_count, row_count, fine_weights.shape[2]
    )
    arrived = lax.all_to_all(fine_send, "grp", split_axis=0, concat_axis=0, tiled=True)
    merged = jnp.sum(arrived, axis=0, dtype=jnp.float32).astype(jnp.bfloat16)
    fine_block = lax.all_to_all(merged, "mem", split_axis=0, concat_axis=1, tiled=True)[0]
    coarse_term, coarse_back = level_terms(tokens, cotangent, coarse_block)
    middle_term, middle_back = level_terms(tokens, cotangent, middle_block)
    fine_term, fine_back = level_terms(tokens, cotangent, fine_block)
    tokens_grad = (coarse_back + middle_back + fine_back).astype(jnp.bfloat16)
    coarse_parts, middle_parts = (
        lax.all_to_all(
            coarse_term.reshape(member_count, row_count, -1),
            "mem",
            split_axis=0,
            concat_axis=0,
            tiled=True,
        ),
        lax.all_to_all(
            middle_term.reshape(member_count, row_count, -1),
            "mem",
            split_axis=0,
            concat_axis=0,
            tiled=True,
        ),
    )
    coarse_local = collect_blocks(coarse_pick, coarse_parts)
    middle_local = collect_blocks(middle_pick, middle_parts)
    coarse_total, middle_total = lax.psum((coarse_local, middle_local), "grp")
    fine_parts = lax.all_to_all(
        fine_term.reshape(member_count, row_count, -1),
        "mem",
        split_axis=0,
        concat_axis=0,
        tiled=True,
    )
    owner_group = group_paths[:, 2] // fine_owned
    destined = (jnp.arange(group_count, dtype=jnp.int32)[:, None] == owner_group[None, :]).astype(
        jnp.float32
    )
    outgoing = destined[:, :, None, None] * fine_parts[None]
    returned = lax.all_to_all(outgoing, "grp", split_axis=0, concat_axis=0, tiled=True)
    fine_local = collect_blocks(
        fine_pick, returned.reshape(group_count * member_count, row_count, -1)
    )
    return (
        tokens_grad,
        coarse_total.astype(jnp.bfloat16),
        middle_total.astype(jnp.bfloat16),
        fine_local.astype(jnp.bfloat16),
    )


def solution(mesh):
    return jax.shard_map(
        on_device,
        mesh=mesh,
        in_specs=(
            P(("grp", "mem"), None),
            P(("grp", "mem"), None),
            P(("grp", "mem"), None),
            P(None, "mem", None),
            P(None, "mem", None),
            P("grp", "mem", None),
        ),
        out_specs=(
            P(("grp", "mem"), None),
            P(None, "mem", None),
            P(None, "mem", None),
            P("grp", "mem", None),
        ),
        check_vma=False,
    )
```

profile of v0, /device:TPU:63, one launch (start us, length us, event | category | flops | bytes accessed | tf_op | source)
XLA Modules:
  0.0 555.5 jit_solution(7141725121758117286)
XLA Ops:
  7.2 104.7 %all-gather = s32[512,1,3]{2,1,0:T(1,128)S(1)} all-gather(s32[1,1,3]{2,1,0:T(1,128)} %bitcast.100), channel_id=1, replica_groups=mesh['grp'=8,'mem'=64] {'grp','mem'}, dimensions={0}, use_global_device_ids=true | all-gather | bytes 6156 | tf_op jit(solution)/shard_map/all_gather | solution.py:54
  113.2 32.7 %all_to_all.43 = bf16[8,64,16,128]{3,1,2,0:T(8,128)(2,1)S(1)} all-to-all(bf16[8,64,16,128]{3,1,2,0:T(8,128)(2,1)S(1)} %copy.78), channel_id=1, replica_groups=mesh['grp'=8,'mem'=64] {'grp'}, dimensions={0} | all-to-all | bytes 4194304 | tf_op jit(solution)/shard_map/all_to_all | solution.py:67
  147.1 12.7 %all-to-all-start.2 = ((bf16[64,16,128]{2,1,0:T(8,128)(2,1)}), bf16[64,16,128]{2,1,0:T(8,128)(2,1)S(1)}, u32[]{:S(2)}, u32[]{:S(2)}) async-start(bf16[64,16,128]{2,1,0:T(8,128)(2,1)} %copy.80), calls=%async_computation.2 | async-start | bytes 524288 | tf_op jit(solution)/shard_map/all_to_all | solution.py:69
  159.9 1.4 convolution_convert_fusion.1
  162.4 16.9 %all-to-all-done.2 = bf16[64,16,128]{2,1,0:T(8,128)(2,1)S(1)} async-done(((bf16[64,16,128]{2,1,0:T(8,128)(2,1)}), bf16[64,16,128]{2,1,0:T(8,128)(2,1)S(1)}, u32[]{:S(2)}, u32[]{:S(2)}) %all-to-all-start.2) | async-done | bytes 262176 | tf_op jit(solution)/shard_map/all_to_all | solution.py:69
  179.3 7.3 %all-to-all-start = ((bf16[64,16,256]{2,1,0:T(8,128)(2,1)}), bf16[64,16,256]{2,1,0:T(8,128)(2,1)S(1)}, u32[]{:S(2)}, u32[]{:S(2)}) async-start(bf16[64,16,256]{2,1,0:T(8,128)(2,1)} %copy.75), calls=%async_computation | async-start | bytes 1048576 | tf_op jit(solution)/shard_map/all_to_all | solution.py:61
  188.6 28.1 %all-to-all-done = bf16[64,16,256]{2,1,0:T(8,128)(2,1)S(1)} async-done(((bf16[64,16,256]{2,1,0:T(8,128)(2,1)}), bf16[64,16,256]{2,1,0:T(8,128)(2,1)S(1)}, u32[]{:S(2)}, u32[]{:S(2)}) %all-to-all-start) | async-done | bytes 524320 | tf_op jit(solution)/shard_map/all_to_all | solution.py:61
  216.7 8.0 %all-to-all-start.5 = ((f32[64,16,128]{2,1,0:T(8,128)}), f32[64,16,128]{2,1,0:T(8,128)}, u32[]{:S(2)}, u32[]{:S(2)}) async-start(f32[64,16,128]{2,1,0:T(8,128)} %bitcast.30), calls=%async_computation.5 | async-start | bytes 1048576 | tf_op jit(solution)/shard_map/all_to_all | solution.py:93
  226.6 1.3 copy.83
  228.0 28.1 %all-to-all-done.5 = f32[64,16,128]{2,1,0:T(8,128)} async-done(((f32[64,16,128]{2,1,0:T(8,128)}), f32[64,16,128]{2,1,0:T(8,128)}, u32[]{:S(2)}, u32[]{:S(2)}) %all-to-all-start.5) | async-done | bytes 524320 | tf_op jit(solution)/shard_map/all_to_all | solution.py:93
  256.0 6.6 %all-to-all-start.4 = ((f32[64,16,256]{2,1,0:T(8,128)}), f32[64,16,256]{2,1,0:T(8,128)S(1)}, u32[]{:S(2)}, u32[]{:S(2)}) async-start(f32[64,16,256]{2,1,0:T(8,128)} %bitcast.25), calls=%async_computation.4 | async-start | bytes 2097152 | tf_op jit(solution)/shard_map/all_to_all | solution.py:82
  263.9 2.6 broadcast_multiply_fusion
  266.5 51.7 %all-to-all-done.4 = f32[64,16,256]{2,1,0:T(8,128)S(1)} async-done(((f32[64,16,256]{2,1,0:T(8,128)}), f32[64,16,256]{2,1,0:T(8,128)S(1)}, u32[]{:S(2)}, u32[]{:S(2)}) %all-to-all-start.4) | async-done | bytes 1048608 | tf_op jit(solution)/shard_map/all_to_all | solution.py:82
  319.2 9.0 %all-to-all-start.6 = ((f32[8,64,16,128]{3,1,2,0:T(8,128)}), f32[8,64,16,128]{3,1,2,0:T(8,128)}, u32[]{:S(2)}, u32[]{:S(2)}) async-start(f32[8,64,16,128]{3,1,2,0:T(8,128)} %broadcast_multiply_fusion), calls=%async_computation.6 | async-start | bytes 8388608 | tf_op jit(solution)/shard_map/all_to_all | solution.py:105
  328.4 50.9 %all-gather.3.cloned.1.call-done = bf16[4,1024,512]{2,1,0:T(8,128)(2,1)} async-done(((bf16[4,16,512]{2,1,0:T(8,128)(2,1)}), bf16[4,1024,512]{2,1,0:T(8,128)(2,1)}) %all-gather.3.cloned.1.call-update) | async-done | bytes 4194320 | tf_op jit(solution)/shard_map/all_gather | solution.py:59
  379.3 1.3 dynamic-slice_bitcast_fusion
  382.0 1.9 copy.81
  383.9 10.2 %all-to-all-start.3 = ((f32[64,16,512]{2,1,0:T(8,128)}), f32[64,16,512]{2,1,0:T(8,128)S(1)}, u32[]{:S(2)}, u32[]{:S(2)}) async-start(f32[64,16,512]{2,1,0:T(8,128)} %bitcast.89), calls=%async_computation.3 | async-start | bytes 4194304 | tf_op jit(solution)/shard_map/all_to_all | solution.py:75
  394.1 3.6 fusion.3
  399.3 2.5 copy.87
  401.8 1.7 convolution_convert_fusion.2
  404.6 81.4 %all-to-all-done.3 = f32[64,16,512]{2,1,0:T(8,128)S(1)} async-done(((f32[64,16,512]{2,1,0:T(8,128)}), f32[64,16,512]{2,1,0:T(8,128)S(1)}, u32[]{:S(2)}, u32[]{:S(2)}) %all-to-all-start.3) | async-done | bytes 2097184 | tf_op jit(solution)/shard_map/all_to_all | solution.py:75
  486.0 2.0 fusion
  488.0 59.0 %all-reduce.2 = (bf16[4,16,512]{2,0,1:T(4,128)(2,1)S(1)}, bf16[64,16,256]{2,0,1:T(8,128)(2,1)S(1)}) all-reduce(f32[4,16,512]{2,0,1:T(4,128)S(1)} %fusion, f32[64,16,256]{2,0,1:T(8,128)} %fusion.3), channel_id=1, replica_groups=mesh['grp'=8,'mem'=64] {'grp'}, use_global_device_ids=true, to_apply=%region_1.2 | all-reduce | flops 294912 | bytes 1769472 | tf_op jit(solution)/shard_map/psum | solution.py:92
  (55 shorter events, 15.5 us)
Async XLA Ops:
  7.2 105.0 %copy-start = (bf16[128,16,128]{2,1,0:T(8,128)(2,1)S(1)}, bf16[128,16,128]{2,1,0:T(8,128)(2,1)}, u32[]{:S(2)}) copy-start(bf16[128,16,128]{2,1,0:T(8,128)(2,1)} %param.11) | copy-start | bytes 1572868
  146.2 40.4 %copy-start.1 = (bf16[128,1024]{1,0:T(8,128)(2,1)S(1)}, bf16[128,1024]{1,0:T(8,128)(2,1)}, u32[]{:S(2)}) copy-start(bf16[128,1024]{1,0:T(8,128)(2,1)} %param.6) | copy-start | bytes 786436
  147.1 39.8 %copy-start.5 = (bf16[128,1024]{1,0:T(8,128)(2,1)S(1)}, bf16[128,1024]{1,0:T(8,128)(2,1)}, u32[]{:S(2)}) copy-start(bf16[128,1024]{1,0:T(8,128)(2,1)} %param.7) | copy-start | bytes 786436
  147.1 32.2 %all-to-all-start.2 = ((bf16[64,16,128]{2,1,0:T(8,128)(2,1)}), bf16[64,16,128]{2,1,0:T(8,128)(2,1)S(1)}, u32[]{:S(2)}, u32[]{:S(2)}) async-start(bf16[64,16,128]{2,1,0:T(8,128)(2,1)} %copy.80), calls=%async_computation.2 | async-start | bytes 524288 | tf_op jit(solution)/shard_map/all_to_all | solution.py:69
  179.3 37.4 %all-to-all-start = ((bf16[64,16,256]{2,1,0:T(8,128)(2,1)}), bf16[64,16,256]{2,1,0:T(8,128)(2,1)S(1)}, u32[]{:S(2)}, u32[]{:S(2)}) async-start(bf16[64,16,256]{2,1,0:T(8,128)(2,1)} %copy.75), calls=%async_computation | async-start | bytes 1048576 | tf_op jit(solution)/shard_map/all_to_all | solution.py:61
  216.7 9.8 %copy-start.6 = (bf16[64,16,256]{2,1,0:T(8,128)(2,1)}, bf16[64,16,256]{2,1,0:T(8,128)(2,1)S(1)}, u32[]{:S(2)}) copy-start(bf16[64,16,256]{2,1,0:T(8,128)(2,1)S(1)} %all-to-all-done) | copy-start | bytes 1572868
  216.7 39.3 %all-to-all-start.5 = ((f32[64,16,128]{2,1,0:T(8,128)}), f32[64,16,128]{2,1,0:T(8,128)}, u32[]{:S(2)}, u32[]{:S(2)}) async-start(f32[64,16,128]{2,1,0:T(8,128)} %bitcast.30), calls=%async_computation.5 | async-start | bytes 1048576 | tf_op jit(solution)/shard_map/all_to_all | solution.py:93
  224.8 154.5 %all-gather.3.cloned.1.call-start = ((), (), s32[]{:S(2)}) async-start(), calls=%async_computation.7 | async-start | bytes 4259840 | tf_op jit(solution)/shard_map/all_gather | solution.py:59
  256.0 62.2 %all-to-all-start.4 = ((f32[64,16,256]{2,1,0:T(8,128)}), f32[64,16,256]{2,1,0:T(8,128)S(1)}, u32[]{:S(2)}, u32[]{:S(2)}) async-start(f32[64,16,256]{2,1,0:T(8,128)} %bitcast.25), calls=%async_computation.4 | async-start | bytes 2097152 | tf_op jit(solution)/shard_map/all_to_all | solution.py:82
  266.5 61.8 %copy-start.8 = (s32[1,3]{1,0:T(1,128)S(1)}, s32[1,3]{1,0:T(1,128)}, u32[]{:S(2)}) copy-start(s32[1,3]{1,0:T(1,128)} %param.8) | copy-start | bytes 40
  318.2 1.0 copy-start.2
  319.2 64.7 %all-to-all-start.6 = ((f32[8,64,16,128]{3,1,2,0:T(8,128)}), f32[8,64,16,128]{3,1,2,0:T(8,128)}, u32[]{:S(2)}, u32[]{:S(2)}) async-start(f32[8,64,16,128]{3,1,2,0:T(8,128)} %broadcast_multiply_fusion), calls=%async_computation.6 | async-start | bytes 8388608 | tf_op jit(solution)/shard_map/all_to_all | solution.py:105
  380.6 1.0 copy-start.3
  383.9 102.1 %all-to-all-start.3 = ((f32[64,16,512]{2,1,0:T(8,128)}), f32[64,16,512]{2,1,0:T(8,128)S(1)}, u32[]{:S(2)}, u32[]{:S(2)}) async-start(f32[64,16,512]{2,1,0:T(8,128)} %bitcast.89), calls=%async_computation.3 | async-start | bytes 4194304 | tf_op jit(solution)/shard_map/all_to_all | solution.py:75
  394.1 3.6 copy-start.4
  394.1 4.0 copy-start.7
Sparse Core Ops, SparseCore 0:
  228.6 150.6 all-gather.2
where the time goes:
time: 556 us
  waiting for transfers between devices  258 us (46%)
  blocking collectives  196 us (35%)
  starting transfers between devices  53.9 us (10%)
  local copies, waits for them, and re-layouts  15.4 us (3%)
  between operations  14.5 us (3%)
  matrix products  14.1 us (3%)
    all_gather x1, blocking collectives, on_device(): all_paths = lax.all_gather(path, ('grp', 'mem'), axis=0, tiled=True)  105 us
    all_to_all x1, waiting for transfers between devices, on_device(): lax.all_to_all(coarse_term.reshape(member_count, row_count, -1), 'mem', s...  81.4 us
    psum x1, blocking collectives, on_device(): coarse_total, middle_total = lax.psum((coarse_local, middle_local), 'grp')  59 us
    all_to_all x1, waiting for transfers between devices, on_device(): lax.all_to_all(middle_term.reshape(member_count, row_count, -1), 'mem', s...  51.7 us
    all_gather x1, waiting for transfers between devices, on_device(): every_block = lax.all_gather(coarse_weights, 'mem', axis=1, tiled=True)  50.9 us
    all_to_all x1, blocking collectives, on_device(): lax.all_to_all(fine_send, 'grp', split_axis=0, concat_axis=0, tiled=True)  32.7 us
    all_to_all x1, waiting for transfers between devices, on_device(): lax.all_to_all(middle_send, 'mem', split_axis=0, concat_axis=1, tiled=True)  28.1 us
    all_to_all x1, waiting for transfers between devices, on_device(): lax.all_to_all(fine_term.reshape(member_count, row_count, -1), 'mem', spl...  28.1 us
  transfers between devices with their start and end apart: 7, of which 6 were waited for; matrix products, arithmetic and copies ran while one was open for 5% of the time, Pallas kernels for 0%

commit v1 on v0

--- a/solution.py
+++ b/solution.py
@@ -56,7 +56,14 @@
     coarse_pick = one_hot_rows(group_paths[:, 0], coarse_weights.shape[0])
     middle_pick = one_hot_rows(group_paths[:, 1], middle_weights.shape[0])
     middle_send = select_blocks(middle_pick, middle_weights)
-    every_block = lax.all_gather(coarse_weights, "mem", axis=1, tiled=True)
+    made = []
+    fan = lax.axis_size("mem")
+    for t in tuple(range(coarse_weights.ndim)):
+        made.append(fan if t == 1 else 1)
+    piece_out = jnp.tile(coarse_weights, made)
+    every_block = lax.all_to_all(
+        piece_out, axis_name="mem", split_axis=1, tiled=True, concat_axis=1
+    )
     coarse_block = lax.dynamic_index_in_dim(every_block, route[0], 0, keepdims=False)
     middle_block = lax.all_to_all(middle_send, "mem", split_axis=0, concat_axis=1, tiled=True)[0]
     offsets = all_paths[:, 2] - group * fine_owned

time: 556 us -> 727 us (1.31)
  the two profiles are of different devices: /device:TPU:63 before, /device:TPU:31 now
where the time goes in v1:
time: 727 us; the launch traced here: 726 us
  waiting for transfers between devices  415 us (57%)
  blocking collectives  200 us (28%)
  starting transfers between devices  70.4 us (10%)
  local copies, waits for them, and re-layouts  21.8 us (3%)
  matrix products  13.9 us (2%)
    all_to_all x1, waiting for transfers between devices, on_device(): lax.all_to_all(piece_out, axis_name='mem', split_axis=1, tiled=True, conc...  177 us
    all_gather x1, blocking collectives, on_device(): all_paths = lax.all_gather(path, ('grp', 'mem'), axis=0, tiled=True)  105 us
    all_to_all x1, waiting for transfers between devices, on_device(): lax.all_to_all(coarse_term.reshape(member_count, row_count, -1), 'mem', s...  80.5 us
    psum x1, blocking collectives, on_device(): coarse_total, middle_total = lax.psum((coarse_local, middle_local), 'grp')  60.9 us
    all_to_all x1, waiting for transfers between devices, on_device(): lax.all_to_all(middle_term.reshape(member_count, row_count, -1), 'mem', s...  50 us
    all_to_all x1, waiting for transfers between devices, on_device(): lax.all_to_all(outgoing, 'grp', split_axis=0, concat_axis=0, tiled=True)  39.1 us
    all_to_all x1, blocking collectives, on_device(): lax.all_to_all(fine_send, 'grp', split_axis=0, concat_axis=0, tiled=True)  34 us
    all_to_all x1, waiting for transfers between devices, on_device(): lax.all_to_all(fine_term.reshape(member_count, row_count, -1), 'mem', spl...  26.6 us
  transfers between devices with their start and end apart: 7, of which 7 were waited for; matrix products, arithmetic and copies ran while one was open for 4% of the time, Pallas kernels for 0%

profile of v1, /device:TPU:31, one launch (start us, length us, event | category | flops | bytes accessed | tf_op | source)
XLA Modules:
  0.0 726.1 jit_solution(5686502105720229815)
XLA Ops:
  0.6 105.3 %all-gather = s32[512,1,3]{2,1,0:T(1,128)S(1)} all-gather(s32[1,1,3]{2,1,0:T(1,128)} %bitcast.106), channel_id=1, replica_groups=mesh['grp'=8,'mem'=64] {'grp','mem'}, dimensions={0}, use_global_device_ids=true | all-gather | bytes 6156 | tf_op jit(solution)/shard_map/all_gather | solution.py:54
  107.2 34.0 %all_to_all.48 = bf16[8,64,16,128]{3,1,2,0:T(8,128)(2,1)S(1)} all-to-all(bf16[8,64,16,128]{3,1,2,0:T(8,128)(2,1)S(1)} %copy.83), channel_id=1, replica_groups=mesh['grp'=8,'mem'=64] {'grp'}, dimensions={0} | all-to-all | bytes 4194304 | tf_op jit(solution)/shard_map/all_to_all | solution.py:74
  142.5 11.3 %all-to-all-start.3 = ((bf16[64,16,128]{2,1,0:T(8,128)(2,1)}), bf16[64,16,128]{2,1,0:T(8,128)(2,1)S(1)}, u32[]{:S(2)}, u32[]{:S(2)}) async-start(bf16[64,16,128]{2,1,0:T(8,128)(2,1)} %copy.85), calls=%async_computation.3 | async-start | bytes 524288 | tf_op jit(solution)/shard_map/all_to_all | solution.py:76
  156.3 16.3 %all-to-all-done.3 = bf16[64,16,128]{2,1,0:T(8,128)(2,1)S(1)} async-done(((bf16[64,16,128]{2,1,0:T(8,128)(2,1)}), bf16[64,16,128]{2,1,0:T(8,128)(2,1)S(1)}, u32[]{:S(2)}, u32[]{:S(2)}) %all-to-all-start.3) | async-done | bytes 262176 | tf_op jit(solution)/shard_map/all_to_all | solution.py:76
  172.6 7.9 %all-to-all-start.1 = ((bf16[64,16,256]{2,1,0:T(8,128)(2,1)}), bf16[64,16,256]{2,1,0:T(8,128)(2,1)S(1)}, u32[]{:S(2)}, u32[]{:S(2)}) async-start(bf16[64,16,256]{2,1,0:T(8,128)(2,1)} %copy.80), calls=%async_computation.1 | async-start | bytes 1048576 | tf_op jit(solution)/shard_map/all_to_all | solution.py:68
  182.5 26.3 %all-to-all-done.1 = bf16[64,16,256]{2,1,0:T(8,128)(2,1)S(1)} async-done(((bf16[64,16,256]{2,1,0:T(8,128)(2,1)}), bf16[64,16,256]{2,1,0:T(8,128)(2,1)S(1)}, u32[]{:S(2)}, u32[]{:S(2)}) %all-to-all-start.1) | async-done | bytes 524320 | tf_op jit(solution)/shard_map/all_to_all | solution.py:68
  208.9 9.8 %all-to-all-start.6 = ((f32[64,16,128]{2,1,0:T(8,128)}), f32[64,16,128]{2,1,0:T(8,128)}, u32[]{:S(2)}, u32[]{:S(2)}) async-start(f32[64,16,128]{2,1,0:T(8,128)} %bitcast.31), calls=%async_computation.6 | async-start | bytes 1048576 | tf_op jit(solution)/shard_map/all_to_all | solution.py:100
  221.1 26.6 %all-to-all-done.6 = f32[64,16,128]{2,1,0:T(8,128)} async-done(((f32[64,16,128]{2,1,0:T(8,128)}), f32[64,16,128]{2,1,0:T(8,128)}, u32[]{:S(2)}, u32[]{:S(2)}) %all-to-all-start.6) | async-done | bytes 524320 | tf_op jit(solution)/shard_map/all_to_all | solution.py:100
  247.7 8.9 %all-to-all-start.5 = ((f32[64,16,256]{2,1,0:T(8,128)}), f32[64,16,256]{2,1,0:T(8,128)S(1)}, u32[]{:S(2)}, u32[]{:S(2)}) async-start(f32[64,16,256]{2,1,0:T(8,128)} %bitcast.26), calls=%async_computation.5 | async-start | bytes 2097152 | tf_op jit(solution)/shard_map/all_to_all | solution.py:89
  256.7 50.0 %all-to-all-done.5 = f32[64,16,256]{2,1,0:T(8,128)S(1)} async-done(((f32[64,16,256]{2,1,0:T(8,128)}), f32[64,16,256]{2,1,0:T(8,128)S(1)}, u32[]{:S(2)}, u32[]{:S(2)}) %all-to-all-start.5) | async-done | bytes 1048608 | tf_op jit(solution)/shard_map/all_to_all | solution.py:89
  306.7 4.0 tile.4
  310.7 10.5 %all-to-all-start = ((bf16[4,1024,512]{2,0,1:T(4,128)(2,1)}), bf16[4,1024,512]{2,0,1:T(4,128)(2,1)}, u32[]{:S(2)}, u32[]{:S(2)}) async-start(bf16[4,1024,512]{2,0,1:T(4,128)(2,1)} %bitcast.90), calls=%async_computation | async-start | bytes 8388608 | tf_op jit(solution)/shard_map/all_to_all | solution.py:64
  322.4 2.6 broadcast_multiply_fusion
  325.0 176.5 %all-to-all-done = bf16[4,1024,512]{2,0,1:T(4,128)(2,1)} async-done(((bf16[4,1024,512]{2,0,1:T(4,128)(2,1)}), bf16[4,1024,512]{2,0,1:T(4,128)(2,1)}, u32[]{:S(2)}, u32[]{:S(2)}) %all-to-all-start) | async-done | bytes 4194336 | tf_op jit(solution)/shard_map/all_to_all | solution.py:64
  501.6 12.8 %all-to-all-start.7 = ((f32[8,64,16,128]{3,1,2,0:T(8,128)}), f32[8,64,16,128]{3,1,2,0:T(8,128)}, u32[]{:S(2)}, u32[]{:S(2)}) async-start(f32[8,64,16,128]{3,1,2,0:T(8,128)} %broadcast_multiply_fusion), calls=%async_computation.7 | async-start | bytes 8388608 | tf_op jit(solution)/shard_map/all_to_all | solution.py:112
  514.5 4.4 constant_dynamic-slice_fusion.1
  520.6 1.9 copy.86
  522.5 39.1 %all-to-all-done.7 = f32[8,64,16,128]{3,1,2,0:T(8,128)} async-done(((f32[8,64,16,128]{3,1,2,0:T(8,128)}), f32[8,64,16,128]{3,1,2,0:T(8,128)}, u32[]{:S(2)}, u32[]{:S(2)}) %all-to-all-start.7) | async-done | bytes 4194336 | tf_op jit(solution)/shard_map/all_to_all | solution.py:112
  561.5 9.1 %all-to-all-start.4 = ((f32[64,16,512]{2,1,0:T(8,128)}), f32[64,16,512]{2,1,0:T(8,128)S(1)}, u32[]{:S(2)}, u32[]{:S(2)}) async-start(f32[64,16,512]{2,1,0:T(8,128)} %bitcast.92), calls=%async_computation.4 | async-start | bytes 4194304 | tf_op jit(solution)/shard_map/all_to_all | solution.py:82
  570.7 3.5 fusion.3
  574.2 2.5 copy.92
  581.0 80.5 %all-to-all-done.4 = f32[64,16,512]{2,1,0:T(8,128)S(1)} async-done(((f32[64,16,512]{2,1,0:T(8,128)}), f32[64,16,512]{2,1,0:T(8,128)S(1)}, u32[]{:S(2)}, u32[]{:S(2)}) %all-to-all-start.4) | async-done | bytes 2097184 | tf_op jit(solution)/shard_map/all_to_all | solution.py:82
  661.5 2.0 fusion
  663.5 60.9 %all-reduce.2 = (bf16[4,16,512]{2,0,1:T(4,128)(2,1)S(1)}, bf16[64,16,256]{2,0,1:T(8,128)(2,1)S(1)}) all-reduce(f32[4,16,512]{2,0,1:T(4,128)S(1)} %fusion, f32[64,16,256]{2,0,1:T(8,128)} %fusion.3), channel_id=1, replica_groups=mesh['grp'=8,'mem'=64] {'grp'}, use_global_device_ids=true, to_apply=%region_1.2 | all-reduce | flops 294912 | bytes 1769472 | tf_op jit(solution)/shard_map/psum | solution.py:99
  (59 shorter events, 18.5 us)
Async XLA Ops:
  0.6 105.5 %copy-start = (bf16[128,16,128]{2,1,0:T(8,128)(2,1)S(1)}, bf16[128,16,128]{2,1,0:T(8,128)(2,1)}, u32[]{:S(2)}) copy-start(bf16[128,16,128]{2,1,0:T(8,128)(2,1)} %param.11) | copy-start | bytes 1572868
  141.6 39.0 %copy-start.1 = (bf16[128,1024]{1,0:T(8,128)(2,1)S(1)}, bf16[128,1024]{1,0:T(8,128)(2,1)}, u32[]{:S(2)}) copy-start(bf16[128,1024]{1,0:T(8,128)(2,1)} %param.6) | copy-start | bytes 786436
  142.5 38.3 %copy-start.5 = (bf16[128,1024]{1,0:T(8,128)(2,1)S(1)}, bf16[128,1024]{1,0:T(8,128)(2,1)}, u32[]{:S(2)}) copy-start(bf16[128,1024]{1,0:T(8,128)(2,1)} %param.7) | copy-start | bytes 786436
  142.5 30.1 %all-to-all-start.3 = ((bf16[64,16,128]{2,1,0:T(8,128)(2,1)}), bf16[64,16,128]{2,1,0:T(8,128)(2,1)S(1)}, u32[]{:S(2)}, u32[]{:S(2)}) async-start(bf16[64,16,128]{2,1,0:T(8,128)(2,1)} %copy.85), calls=%async_computation.3 | async-start | bytes 524288 | tf_op jit(solution)/shard_map/all_to_all | solution.py:76
  172.6 36.3 %all-to-all-start.1 = ((bf16[64,16,256]{2,1,0:T(8,128)(2,1)}), bf16[64,16,256]{2,1,0:T(8,128)(2,1)S(1)}, u32[]{:S(2)}, u32[]{:S(2)}) async-start(bf16[64,16,256]{2,1,0:T(8,128)(2,1)} %copy.80), calls=%async_computation.1 | async-start | bytes 1048576 | tf_op jit(solution)/shard_map/all_to_all | solution.py:68
  208.9 10.9 %copy-start.6 = (bf16[64,16,256]{2,1,0:T(8,128)(2,1)}, bf16[64,16,256]{2,1,0:T(8,128)(2,1)S(1)}, u32[]{:S(2)}) copy-start(bf16[64,16,256]{2,1,0:T(8,128)(2,1)S(1)} %all-to-all-done.1) | copy-start | bytes 1572868
  208.9 38.8 %all-to-all-start.6 = ((f32[64,16,128]{2,1,0:T(8,128)}), f32[64,16,128]{2,1,0:T(8,128)}, u32[]{:S(2)}, u32[]{:S(2)}) async-start(f32[64,16,128]{2,1,0:T(8,128)} %bitcast.31), calls=%async_computation.6 | async-start | bytes 1048576 | tf_op jit(solution)/shard_map/all_to_all | solution.py:100
  219.8 36.8 %copy-start.8 = (bf16[4,16,512]{2,1,0:T(8,128)(2,1)S(1)}, bf16[4,16,512]{2,1,0:T(8,128)(2,1)}, u32[]{:S(2)}) copy-start(bf16[4,16,512]{2,1,0:T(8,128)(2,1)} %param.9) | copy-start | bytes 196612
  247.7 59.0 %all-to-all-start.5 = ((f32[64,16,256]{2,1,0:T(8,128)}), f32[64,16,256]{2,1,0:T(8,128)S(1)}, u32[]{:S(2)}, u32[]{:S(2)}) async-start(f32[64,16,256]{2,1,0:T(8,128)} %bitcast.26), calls=%async_computation.5 | async-start | bytes 2097152 | tf_op jit(solution)/shard_map/all_to_all | solution.py:89
  306.7 4.0 copy-start.2
  310.7 190.9 %all-to-all-start = ((bf16[4,1024,512]{2,0,1:T(4,128)(2,1)}), bf16[4,1024,512]{2,0,1:T(4,128)(2,1)}, u32[]{:S(2)}, u32[]{:S(2)}) async-start(bf16[4,1024,512]{2,0,1:T(4,128)(2,1)} %bitcast.90), calls=%async_computation | async-start | bytes 8388608 | tf_op jit(solution)/shard_map/all_to_all | solution.py:64
  325.0 189.3 %copy-start.9 = (s32[1,3]{1,0:T(1,128)S(1)}, s32[1,3]{1,0:T(1,128)}, u32[]{:S(2)}) copy-start(s32[1,3]{1,0:T(1,128)} %param.8) | copy-start | bytes 40
  501.6 60.0 %all-to-all-start.7 = ((f32[8,64,16,128]{3,1,2,0:T(8,128)}), f32[8,64,16,128]{3,1,2,0:T(8,128)}, u32[]{:S(2)}, u32[]{:S(2)}) async-start(f32[8,64,16,128]{3,1,2,0:T(8,128)} %broadcast_multiply_fusion), calls=%async_computation.7 | async-start | bytes 8388608 | tf_op jit(solution)/shard_map/all_to_all | solution.py:112
  519.1 1.0 copy-start.3
  561.5 100.0 %all-to-all-start.4 = ((f32[64,16,512]{2,1,0:T(8,128)}), f32[64,16,512]{2,1,0:T(8,128)S(1)}, u32[]{:S(2)}, u32[]{:S(2)}) async-start(f32[64,16,512]{2,1,0:T(8,128)} %bitcast.92), calls=%async_computation.4 | async-start | bytes 4194304 | tf_op jit(solution)/shard_map/all_to_all | solution.py:82
  576.7 2.8 copy-start.4
  578.4 1.5 copy-start.7
